TPU v7x, 32 devices: a whole 2x2x4 slice. The times are simulated.
32 devices in a mesh: wide: 16 (over z, x, core), narrow: 2 (over y).
Axes of the slice: x: 2, y: 2, z: 4, core: 2. Of those that a mesh axis runs over, the one named last changes fastest.
Arguments:
- tensor: bfloat16 [16, 4096, 2048], P(None, 'wide', 'narrow'), may hold values from -100 to 100
- first_factor: bfloat16 [16, 256], replicated, may hold values from -8 to 8
- third_factor: bfloat16 [2048, 256], P('narrow'), may hold values from -10 to 10
Outputs:
- second_factor: bfloat16 [4096, 256], P('wide')
- third_new: bfloat16 [2048, 256], P('narrow')
- first_mode: float32 [16, 256], replicated
All inputs are finite; a program needn't handle non-finite values.
Results may differ from a plain program's by a relative error of at most 0.008.
Values may be sent and summed in bfloat16 or wider, within the bound.
A program may use at most 128 MiB of HBM per device.

v0:
```python
import math

import jax
import jax.numpy as jnp
from jax import lax
from jax.sharding import PartitionSpec as P

ridge = 0.5


def solve_rows(rows, system):
    lower = jnp.linalg.cholesky(system)
    return jax.scipy.linalg.cho_solve((lower, True), rows.T).T


def on_device(tensor, first_factor, third_factor):
    window, second_local, third_local = tensor.shape
    rank = first_factor.shape[1]
    second_total = second_local * lax.axis_size("wide")
    third_total = third_local * lax.axis_size("narrow")
    first_wide = first_factor.astype(jnp.float32)
    identity = jnp.eye(rank, dtype=jnp.float32)
    gram_first = jnp.dot(first_factor.T, first_factor, preferred_element_type=jnp.float32) / window
    gram_part = jnp.dot(third_factor.T, third_factor, preferred_element_type=jnp.float32)
    gram_third = lax.psum(gram_part, "narrow") / third_total
    system_second = gram_first * gram_third + ridge * identity
    contracted = jnp.dot(
        tensor.reshape(window * second_local, third_local),
        third_factor,
        preferred_element_type=jnp.float32,
    )
    contracted = contracted.reshape(window, second_local, rank)
    partial_second = jnp.einsum(
        "ijr,ir->jr", contracted, first_wide, precision=lax.Precision.HIGHEST
    ) / math.sqrt(window * third_total)
    mttkrp_second = lax.psum(partial_second, "narrow")
    second_factor = solve_rows(mttkrp_second, system_second).astype(jnp.bfloat16)
    gram_local = jnp.dot(second_factor.T, second_factor, preferred_element_type=jnp.float32)
    gram_second = lax.psum(gram_local, "wide") / second_total
    system_third = gram_first * gram_second + ridge * identity
    middle = jnp.einsum("ijk,jr->ikr", tensor, second_factor, preferred_element_type=jnp.float32)
    partial_third = jnp.einsum(
        "ikr,ir->kr", middle, first_wide, precision=lax.Precision.HIGHEST
    ) / math.sqrt(window * second_total)
    mttkrp_third = lax.psum(partial_third, "wide")
    third_solution = solve_rows(mttkrp_third, system_third)
    third_new = third_solution.astype(jnp.bfloat16)
    partial_first = jnp.einsum(
        "ikr,kr->ir", middle, third_solution, precision=lax.Precision.HIGHEST
    ) / math.sqrt(second_total * third_total)
    first_mode = lax.psum(partial_first, ("wide", "narrow"))
    return (second_factor, third_new, first_mode)


def solution(mesh):
    in_specs = (P(None, "wide", "narrow"), P(), P("narrow", None))
    out_specs = (P("wide", None), P("narrow", None), P())
    return jax.shard_map(
        on_device, mesh=mesh, in_specs=in_specs, out_specs=out_specs, check_vma=False
    )
```

profile of v0, /device:TPU:0, one launch (start us, length us, event | category | flops | bytes accessed | tf_op | source)
XLA Modules:
  0.0 380.9 jit_solution(15535652503810598091)
XLA Ops:
  9.3 5.7 %multiply_reduce_fusion = f32[256,256]{0,1:T(8,128)S(1)} fusion(bf16[16,256,1024]{2,1,0:T(8,128)(2,1)} %param.4, f32[256,16]{0,1:T(8,128)S(1)} %bitcast_convert_fusion.1, bf16[1024,256]{1,0:T(8,128)(2,1)S(1)} %copy-done), kind=kOutput, calls=%fused_computation.9 | convolution fusion | flops 2149515264 | bytes 9191424 | tf_op jit(solution)/shard_map/dot_general | solution.py:27
  16.6 31.0 %all-reduce.8.cloned.1.call-done = (f32[256,256]{1,0:T(8,128)}, f32[256,256]{0,1:T(8,128)}) async-done(((f32[256,256]{1,0:T(8,128)}, f32[256,256]{0,1:T(8,128)}), (f32[256,256]{1,0:T(8,128)}, f32[256,256]{0,1:T(8,128)})) %all-reduce.8.cloned.1.call-update) | async-done | bytes 524304 | tf_op jit(solution)/shard_map/psum | solution.py:36
  48.9 11.7 %cholesky.130 = f32[128,128]{1,0:T(8,128)S(1)} custom-call(f32[128,128]{1,0:T(8,128)S(1)} %cholesky.194), custom_call_target="Cholesky" | custom-call | tf_op jit(solution)/shard_map/jit(cholesky)/cholesky | solution.py:12
  60.7 9.8 %custom-call.25 = f32[1,128,128]{1,2,0:T(8,128)S(1)} custom-call(f32[1,128,128]{2,1,0:T(8,128)S(1)} %get-tuple-element.58), custom_call_target="InvertDiagBlocksLowerTriangular" | custom-call | tf_op jit(solution)/shard_map/jit(cholesky)/cholesky | solution.py:12
  71.0 11.7 %cholesky.147 = f32[128,128]{1,0:T(8,128)S(1)} custom-call(f32[128,128]{1,0:T(8,128)S(1)} %convolution_subtract_fusion.5), custom_call_target="Cholesky" | custom-call | tf_op jit(solution)/shard_map/jit(cholesky)/cholesky | solution.py:12
  85.2 4.4 %while.2 = (s32[]{:T(128)}, f32[256,256]{0,1:T(8,128)S(1)}, s32[2,2]{1,0:T(2,128)S(1)}, f32[2,128,128]{2,1,0:T(8,128)S(1)}, s32[]{:T(128)}) while((s32[]{:T(128)}, f32[256,256]{0,1:T(8,128)S(1)}, s32[2,2]{1,0:T(2,128)S(1)}, f32[2,128,128]{2,1,0:T(8,128)S(1)}, s32[]{:T(128)}) %tuple.46), condition=%wide.while_cond, body=%wide.while_body.sunk | while | flops 2 | bytes 393321 | solution.py:13
  86.0 1.4 dynamic-slice.13
  88.1 1.4 dynamic-slice.13
  89.6 19.7 %custom-call.22 = f32[2,128,128]{1,2,0:T(8,128)S(1)} custom-call(f32[2,128,128]{2,1,0:T(8,128)S(1)} %get-tuple-element.11), custom_call_target="InvertDiagBlocksLowerTriangular" | custom-call | tf_op jit(solution)/shard_map/jit(_cho_solve)/triangular_solve | solution.py:13
  112.8 5.7 %convolution_bitcast_fusion = f32[16,1024,256]{1,2,0:T(8,128)S(1)} fusion(bf16[16,256,1024]{2,1,0:T(8,128)(2,1)} %param.4, bf16[128,256]{1,0:T(8,128)(2,1)S(1)} %get-tuple-element.61, bf16[128,256]{1,0:T(8,128)(2,1)S(1)} %convolution_convert_fusion), kind=kOutput, calls=%fused_computation.8 | convolution fusion | flops 2147745792 | bytes 25296896 | tf_op jit(solution)/shard_map/ijk,jr->ikr/dot_general | solution.py:41
  119.7 4.6 %copy-done.1 = f32[16,1024,256]{1,2,0:T(8,128)} copy-done((f32[16,1024,256]{1,2,0:T(8,128)}, f32[16,1024,256]{1,2,0:T(8,128)S(1)}, u32[]{:S(2)}) %copy-start.1) | copy-done | bytes 16777240
  124.3 13.3 %fusion.2 = f32[256,1,1024]{2,1,0:T(1,128)S(1)} fusion(bf16[16,256,1]{0,2,1:T(2,128)(2,1)S(1)} %copy.32, f32[16,1024,256]{1,2,0:T(8,128)S(1)} %convolution_bitcast_fusion), kind=kOutput, calls=%fused_computation.6 | convolution fusion | flops 50331648 | bytes 17833984 | tf_op jit(solution)/shard_map/ikr,ir->kr/dot_general | solution.py:42
  139.7 93.1 %all-reduce.6.cloned.1.call-done = (f32[256,1024]{1,0:T(8,128)}, f32[256,256]{0,1:T(8,128)}) async-done(((f32[256,1024]{1,0:T(8,128)}, f32[256,256]{0,1:T(8,128)}), (f32[256,1024]{1,0:T(8,128)}, f32[256,256]{0,1:T(8,128)})) %all-reduce.6.cloned.1.call-update) | async-done | bytes 1310736 | tf_op jit(solution)/shard_map/psum | solution.py:45
  234.0 11.7 %cholesky.164 = f32[128,128]{1,0:T(8,128)S(1)} custom-call(f32[128,128]{1,0:T(8,128)S(1)} %cholesky.197), custom_call_target="Cholesky" | custom-call | tf_op jit(solution)/shard_map/jit(cholesky)/cholesky | solution.py:12
  245.7 9.8 %custom-call.26 = f32[1,128,128]{1,2,0:T(8,128)S(1)} custom-call(f32[1,128,128]{2,1,0:T(8,128)S(1)} %get-tuple-element.56), custom_call_target="InvertDiagBlocksLowerTriangular" | custom-call | tf_op jit(solution)/shard_map/jit(cholesky)/cholesky | solution.py:12
  256.0 11.7 %cholesky.181 = f32[128,128]{1,0:T(8,128)S(1)} custom-call(f32[128,128]{1,0:T(8,128)S(1)} %convolution_subtract_fusion.4), custom_call_target="Cholesky" | custom-call | tf_op jit(solution)/shard_map/jit(cholesky)/cholesky | solution.py:12
  270.7 4.1 %while.3 = (s32[]{:T(128)}, f32[256,256]{0,1:T(8,128)S(1)}, s32[2,2]{1,0:T(2,128)S(1)}, f32[2,128,128]{2,1,0:T(8,128)S(1)}, s32[]{:T(128)}) while((s32[]{:T(128)}, f32[256,256]{0,1:T(8,128)S(1)}, s32[2,2]{1,0:T(2,128)S(1)}, f32[2,128,128]{2,1,0:T(8,128)S(1)}, s32[]{:T(128)}) %tuple.58), condition=%wide.while_cond.1, body=%wide.while_body.1.sunk | while | flops 2 | bytes 393321 | solution.py:13
  271.3 1.3 dynamic-slice.15
  273.3 1.3 dynamic-slice.15
  274.8 19.8 %custom-call.23 = f32[2,128,128]{1,2,0:T(8,128)S(1)} custom-call(f32[2,128,128]{2,1,0:T(8,128)S(1)} %get-tuple-element.19), custom_call_target="InvertDiagBlocksLowerTriangular" | custom-call | tf_op jit(solution)/shard_map/jit(_cho_solve)/triangular_solve | solution.py:13
  294.6 1.7 fusion.6
  296.3 1.7 convolution_subtract_fusion.1
  300.6 32.0 %fusion = f32[256,1,16]{2,1,0:T(1,128)S(1)} fusion(f32[16,1024,256]{1,2,0:T(8,128)} %copy-done.1, f32[1024,256,1]{0,1,2:T(8,128)S(1)} %fusion.5), kind=kOutput, calls=%fused_computation.4 | convolution fusion | flops 50331648 | bytes 17842176 | tf_op jit(solution)/shard_map/ikr,kr->ir/dot_general | solution.py:48
  332.6 40.2 %psum.39 = f32[16,256]{1,0:T(8,128)} all-reduce(f32[16,256]{1,0:T(8,128)S(1)} %fusion.31), channel_id=1, replica_groups=mesh['wide'=16,'narrow'=2] {'wide','narrow'}, use_global_device_ids=true, to_apply=%region_8.10 | all-reduce | flops 4096 | bytes 32768 | tf_op jit(solution)/shard_map/psum | solution.py:51
  (86 shorter events, 23.1 us)
Async XLA Ops:
  7.2 1.1 copy-start
  7.2 9.3 %copy-start.2 = (bf16[16,256]{1,0:T(8,128)(2,1)S(1)}, bf16[16,256]{1,0:T(8,128)(2,1)}, u32[]{:S(2)}) copy-start(bf16[16,256]{1,0:T(8,128)(2,1)} %param.5) | copy-start | bytes 24580
  7.2 40.4 %all-reduce.8.cloned.1.call-start = ((), (), s32[]{:S(2)}) async-start(), calls=%async_computation.1 | async-start | bytes 1048576 | tf_op jit(solution)/shard_map/psum | solution.py:36
  15.9 216.9 %all-reduce.6.cloned.1.call-start = ((), (), s32[]{:S(2)}) async-start(), calls=%async_computation | async-start | bytes 2621440 | tf_op jit(solution)/shard_map/psum | solution.py:45
  118.5 5.8 %copy-start.1 = (f32[16,1024,256]{1,2,0:T(8,128)}, f32[16,1024,256]{1,2,0:T(8,128)S(1)}, u32[]{:S(2)}) copy-start(f32[16,1024,256]{1,2,0:T(8,128)S(1)} %convolution_bitcast_fusion) | copy-start | bytes 50331652
Sparse Core Ops, SparseCore 0:
  16.0 31.4 all-reduce.7
  139.0 93.7 all-reduce.5
where the time goes:
time: 384 us; the launch traced here: 381 us
  waiting for transfers between devices  124 us (32%)
  other arithmetic  112 us (29%)
  matrix products  70.3 us (18%)
  blocking collectives  40.2 us (10%)
  between operations  17.1 us (4%)
  local copies, waits for them, and re-layouts  16.1 us (4%)
    psum x1, waiting for transfers between devices, on_device(): mttkrp_third = lax.psum(partial_third, 'wide')  93.1 us
    another operation x13, other arithmetic, solve_rows(): lower = jnp.linalg.cholesky(system)  68.6 us
    psum x1, blocking collectives, on_device(): first_mode = lax.psum(partial_first, ('wide', 'narrow'))  40.2 us
    another operation x5, other arithmetic, solve_rows(): return jax.scipy.linalg.cho_solve((lower, True), rows.T).T  39.6 us
    dot_general x1, matrix products, on_device(): jnp.einsum('ikr,kr->ir', middle, third_solution, precision=lax.Precision....  32 us
    psum x1, waiting for transfers between devices, on_device(): mttkrp_second = lax.psum(partial_second, 'narrow')  31 us
    dot_general x1, matrix products, on_device(): jnp.einsum('ikr,ir->kr', middle, first_wide, precision=lax.Precision.HIGH...  13.3 us
    another operation x12, matrix products, solve_rows(): return jax.scipy.linalg.cho_solve((lower, True), rows.T).T  9.24 us
  transfers between devices with their start and end apart: 2, of which 2 were waited for; matrix products, arithmetic and copies ran while one was open for 0% of the time, Pallas kernels for 0%

commit v1 on v0

v1 whole, which is shorter than its diff:
```python
import functools
import math

import jax
import jax.numpy as jnp
from jax import lax
from jax.experimental import pallas as pl
from jax.experimental.pallas import tpu as pltpu
from jax.sharding import PartitionSpec as P

ridge = 0.5
F32 = jnp.float32
BF16 = jnp.bfloat16
HIGH = lax.Precision.HIGHEST
VM = pl.BlockSpec(memory_space=pltpu.VMEM)
MESH = pl.DeviceIdType.MESH


def params(**more):
    return pltpu.CompilerParams(vmem_limit_bytes=50 * 2**20, **more)


def remote(src, dst, sems, slot, wide, narrow):
    copy = pltpu.make_async_remote_copy(
        src_ref=src, dst_ref=dst, send_sem=sems.at[0, slot], recv_sem=sems.at[1, slot],
        device_id=(wide, narrow), device_id_type=MESH,
    )
    copy.start()
    return copy


def greet(partners):
    barrier = pltpu.get_barrier_semaphore()
    for partner in partners:
        pl.semaphore_signal(barrier, inc=1, device_id=partner, device_id_type=MESH)
    pl.semaphore_wait(barrier, len(partners))


def wait_all(copies):
    for copy in copies:
        copy.wait()


def second_kernel(t_ref, u_ref, w_ref, out_ref):
    step = pl.program_id(0)
    rank = w_ref.shape[1]

    @pl.when(step == 0)
    def _():
        out_ref[pl.ds(0, rank), :] = lax.dot_general(
            w_ref[...], w_ref[...], (((0,), (0,)), ((), ())), preferred_element_type=F32
        )
        out_ref[pl.ds(rank, t_ref.shape[1]), :] = jnp.zeros((t_ref.shape[1], rank), F32)

    out_ref[pl.ds(rank, t_ref.shape[1]), :] += u_ref[0] * jnp.dot(
        t_ref[0], w_ref[...], preferred_element_type=F32
    )


def second_products(tensor, first_wide, third):
    window, rows, depth = tensor.shape
    rank = third.shape[1]
    return pl.pallas_call(
        second_kernel,
        grid=(window,),
        in_specs=[
            pl.BlockSpec((1, rows, depth), lambda i: (i, 0, 0)),
            pl.BlockSpec((1, 1, rank), lambda i: (i, 0, 0)),
            pl.BlockSpec((depth, rank), lambda i: (0, 0)),
        ],
        out_specs=pl.BlockSpec((rank + rows, rank), lambda i: (0, 0)),
        out_shape=jax.ShapeDtypeStruct((rank + rows, rank), F32),
        compiler_params=params(),
    )(tensor, first_wide, third)


def narrow_kernel(count, x_ref, out_ref, land, sems):
    wide, narrow = lax.axis_index("wide"), lax.axis_index("narrow")
    others = [lax.rem(narrow + d, count) for d in range(1, count)]
    greet([(wide, other) for other in others])
    wait_all([remote(x_ref, land.at[d], sems, d, wide, other) for d, other in enumerate(others)])
    out_ref[...] = x_ref[...]
    for d in range(count - 1):
        out_ref[...] += land[d]


def narrow_sum(x, count):
    return pl.pallas_call(
        functools.partial(narrow_kernel, count),
        in_specs=[VM],
        out_specs=VM,
        out_shape=jax.ShapeDtypeStruct(x.shape, F32),
        scratch_shapes=[
            pltpu.VMEM((count - 1,) + x.shape, F32),
            pltpu.SemaphoreType.DMA((2, count - 1)),
        ],
        compiler_params=params(collective_id=0, has_side_effects=True),
    )(x)


def third_kernel(t_ref, u_ref, v_ref, mid_ref, out_ref):
    step = pl.program_id(0)
    part = lax.dot_general(
        t_ref[0], v_ref[...], (((0,), (0,)), ((), ())), preferred_element_type=F32
    )
    mid_ref[0] = part

    @pl.when(step == 0)
    def _():
        out_ref[...] = u_ref[0] * part

    @pl.when(step > 0)
    def _():
        out_ref[...] += u_ref[0] * part


def third_products(tensor, first_wide, second):
    window, rows, depth = tensor.shape
    rank = second.shape[1]
    return pl.pallas_call(
        third_kernel,
        grid=(window,),
        in_specs=[
            pl.BlockSpec((1, rows, depth), lambda i: (i, 0, 0)),
            pl.BlockSpec((1, 1, rank), lambda i: (i, 0, 0)),
            pl.BlockSpec((rows, rank), lambda i: (0, 0)),
        ],
        out_specs=[
            pl.BlockSpec((1, depth, rank), lambda i: (i, 0, 0)),
            pl.BlockSpec((depth, rank), lambda i: (0, 0)),
        ],
        out_shape=[
            jax.ShapeDtypeStruct((window, depth, rank), F32),
            jax.ShapeDtypeStruct((depth, rank), F32),
        ],
        compiler_params=params(),
    )(tensor, first_wide, second)


def place(size):
    wide, narrow = lax.axis_index("wide"), lax.axis_index("narrow")
    chips = size // 2
    chip, core = wide // 2, lax.rem(wide, 2)
    peer = chip * 2 + 1 - core
    others = [lax.rem(chip + d, chips) for d in range(1, chips)]
    return wide, narrow, chips, chip, core, peer, others


def wide_kernel(size, gram_ref, prod_ref, gram_out, prod_out,
                gram_land, prod_land, gram_acc, prod_acc, gram_parts, prod_parts,
                core_sems, gram_sems, prod_sems, share_sems):
    wide, narrow, chips, chip, core, peer, others = place(size)
    greet([(peer, narrow)] + [(other * 2 + core, narrow) for other in others])
    g_half, p_half = gram_ref.shape[0] // 2, prod_ref.shape[0] // 2
    g_rows, p_rows = g_half // chips, p_half // chips

    def part(ref, index, rows):
        return ref.at[pl.ds(pl.multiple_of(index * rows, rows), rows)]

    first = remote(part(gram_ref, 1 - core, g_half), gram_land, core_sems, 0, peer, narrow)
    next_ = remote(part(prod_ref, 1 - core, p_half), prod_land, core_sems, 1, peer, narrow)
    first.wait()
    gram_acc[...] = part(gram_ref, core, g_half)[...] + gram_land[...]
    grams = [remote(part(gram_acc, other, g_rows), gram_parts.at[d], gram_sems, d,
                    other * 2 + core, narrow) for d, other in enumerate(others)]
    next_.wait()
    prod_acc[...] = part(prod_ref, core, p_half)[...] + prod_land[...]
    wait_all(grams)
    total = part(gram_acc, chip, g_rows)[...]
    for d in range(chips - 1):
        total += gram_parts[d]
    mine = part(gram_out, core * chips + chip, g_rows)
    mine[...] = total
    shares = [remote(mine, mine, share_sems, d, other * 2 + core, narrow)
              for d, other in enumerate(others)]
    prods = [remote(part(prod_acc, other, p_rows), prod_parts.at[d], prod_sems, d,
                    other * 2 + core, narrow) for d, other in enumerate(others)]
    wait_all(shares)
    half = part(gram_out, core, g_half)
    last = remote(half, half, core_sems, 2, peer, narrow)
    wait_all(prods)
    total = part(prod_acc, chip, p_rows)[...]
    for d in range(chips - 1):
        total += prod_parts[d]
    prod_out[...] = total
    last.wait()


def wide_sums(gram, prod, size):
    rank = gram.shape[1]
    chips = size // 2
    g_half, p_half = gram.shape[0] // 2, prod.shape[0] // 2
    g_rows, p_rows = g_half // chips, p_half // chips
    return pl.pallas_call(
        functools.partial(wide_kernel, size),
        in_specs=[VM, VM],
        out_specs=[VM, VM],
        out_shape=[
            jax.ShapeDtypeStruct(gram.shape, F32),
            jax.ShapeDtypeStruct((p_rows, rank), F32),
        ],
        scratch_shapes=[
            pltpu.VMEM((g_half, rank), F32),
            pltpu.VMEM((p_half, rank), F32),
            pltpu.VMEM((g_half, rank), F32),
            pltpu.VMEM((p_half, rank), F32),
            pltpu.VMEM((chips - 1, g_rows, rank), F32),
            pltpu.VMEM((chips - 1, p_rows, rank), F32),
            pltpu.SemaphoreType.DMA((2, 3)),
            pltpu.SemaphoreType.DMA((2, chips - 1)),
            pltpu.SemaphoreType.DMA((2, chips - 1)),
            pltpu.SemaphoreType.DMA((2, chips - 1)),
        ],
        compiler_params=params(collective_id=1, has_side_effects=True),
    )(gram, prod)


def gather_kernel(size, x_ref, out_ref, sems, core_sems):
    wide, narrow, chips, chip, core, peer, others = place(size)
    greet([(peer, narrow)] + [(other * 2 + core, narrow) for other in others])
    rows = x_ref.shape[0]
    half = rows * chips
    mine = out_ref.at[pl.ds(pl.multiple_of((core * chips + chip) * rows, rows), rows)]
    copies = [remote(x_ref, mine, sems, d, other * 2 + core, narrow)
              for d, other in enumerate(others)]
    mine[...] = x_ref[...]
    wait_all(copies)
    side = out_ref.at[pl.ds(pl.multiple_of(core * half, half), half)]
    remote(side, side, core_sems, 0, peer, narrow).wait()


def gather_rows(x, size):
    return pl.pallas_call(
        functools.partial(gather_kernel, size),
        in_specs=[VM],
        out_specs=VM,
        out_shape=jax.ShapeDtypeStruct((x.shape[0] * size, x.shape[1]), x.dtype),
        scratch_shapes=[
            pltpu.SemaphoreType.DMA((2, size // 2 - 1)),
            pltpu.SemaphoreType.DMA((2, 1)),
        ],
        compiler_params=params(collective_id=2, has_side_effects=True),
    )(x)


def first_kernel(mid_ref, z_ref, out_ref):
    out_ref[0] = jnp.sum(mid_ref[0] * z_ref[...].astype(F32), axis=0, keepdims=True)


def first_products(middle, third_new):
    window, depth, rank = middle.shape
    return pl.pallas_call(
        first_kernel,
        grid=(window,),
        in_specs=[
            pl.BlockSpec((1, depth, rank), lambda i: (i, 0, 0)),
            pl.BlockSpec((depth, rank), lambda i: (0, 0)),
        ],
        out_specs=pl.BlockSpec((1, 1, rank), lambda i: (i, 0, 0)),
        out_shape=jax.ShapeDtypeStruct((window, 1, rank), F32),
        compiler_params=params(),
    )(middle, third_new)


def total_kernel(size, count, x_ref, out_ref, land, acc, parts, core_sems, sems):
    wide, narrow, chips, chip, core, peer, others = place(size)
    partners = []
    for d in range(chips):
        for e in range(count):
            if d or e:
                partners.append((lax.rem(chip + d, chips) * 2 + core, lax.rem(narrow + e, count)))
    greet([(peer, narrow)] + partners)
    half = x_ref.shape[0] // 2
    theirs = x_ref.at[pl.ds(pl.multiple_of((1 - core) * half, half), half)]
    mine = pl.ds(pl.multiple_of(core * half, half), half)
    remote(theirs, land, core_sems, 0, peer, narrow).wait()
    acc[...] = x_ref[mine, :] + land[...]
    wait_all([remote(acc, parts.at[d], sems, d, *partner) for d, partner in enumerate(partners)])
    total = acc[...]
    for d in range(len(partners)):
        total += parts[d]
    out_ref[mine, :] = total
    remote(out_ref.at[mine], out_ref.at[mine], core_sems, 1, peer, narrow).wait()


def total_sum(x, size, count):
    partners = size // 2 * count - 1
    half = (x.shape[0] // 2, x.shape[1])
    return pl.pallas_call(
        functools.partial(total_kernel, size, count),
        in_specs=[VM],
        out_specs=VM,
        out_shape=jax.ShapeDtypeStruct(x.shape, F32),
        scratch_shapes=[
            pltpu.VMEM(half, F32),
            pltpu.VMEM(half, F32),
            pltpu.VMEM((partners,) + half, F32),
            pltpu.SemaphoreType.DMA((2, 2)),
            pltpu.SemaphoreType.DMA((2, partners)),
        ],
        compiler_params=params(collective_id=3, has_side_effects=True),
    )(x)


def solve_rows(rows, system):
    lower = jnp.linalg.cholesky(system)
    return jax.scipy.linalg.cho_solve((lower, True), rows.T).T


def on_device(size, count, tensor, first_factor, third_factor):
    window, second_local, third_local = tensor.shape
    rank = first_factor.shape[1]
    second_total = second_local * size
    third_total = third_local * count
    first_wide = first_factor.astype(F32).reshape(window, 1, rank)
    identity = jnp.eye(rank, dtype=F32)
    gram_first = jnp.dot(first_factor.T, first_factor, preferred_element_type=F32) / window
    sums = narrow_sum(second_products(tensor, first_wide, third_factor), count)
    gram_third = sums[:rank] / third_total
    mttkrp_second = sums[rank:] / math.sqrt(window * third_total)
    system_second = gram_first * gram_third + ridge * identity
    second_factor = solve_rows(mttkrp_second, system_second).astype(BF16)
    gram_local = jnp.dot(second_factor.T, second_factor, preferred_element_type=F32)
    middle, partial_third = third_products(tensor, first_wide, second_factor)
    gram_second, rows_third = wide_sums(gram_local, partial_third, size)
    system_third = gram_first * (gram_second / second_total) + ridge * identity
    mttkrp_third = rows_third / math.sqrt(window * second_total)
    third_rows = solve_rows(mttkrp_third, system_third).astype(BF16)
    third_new = gather_rows(third_rows, size)
    partial_first = first_products(middle, third_new).reshape(window, rank)
    first_mode = total_sum(partial_first, size, count) / math.sqrt(second_total * third_total)
    return (second_factor, third_new, first_mode)


def solution(mesh):
    size, count = mesh.shape["wide"], mesh.shape["narrow"]
    in_specs = (P(None, "wide", "narrow"), P(), P("narrow", None))
    out_specs = (P("wide", None), P("narrow", None), P())
    return jax.shard_map(
        functools.partial(on_device, size, count), mesh=mesh,
        in_specs=in_specs, out_specs=out_specs, check_vma=False,
    )
```

time: 384 us -> 234 us (0.61)
  waiting for transfers between devices: 124 us -> 0 us
  Pallas kernels: 0 us -> 103 us
  matrix products: 70.3 us -> 5.5 us
  blocking collectives: 40.2 us -> 0 us
  between operations: 17.1 us -> 3.68 us
  local copies, waits for them, and re-layouts: 16.1 us -> 12.1 us
    psum x2 -> x0, waiting for transfers between devices: 124 us -> none  [the longest x1 93.1 us: on_device(): mttkrp_third = lax.psum(partial_third, 'wide')]
    pallas_call x0 -> x7, Pallas kernels: none -> 103 us  [the longest x1 24.5 us: wide_sums(): pl.pallas_call(functools.partial(wide_kernel, size), in_specs=[VM, VM], o...]
    dot_general x7 -> x2, matrix products: 60.1 us -> 1.23 us  [the longest x1 1 us: on_device(): jnp.dot(first_factor.T, first_factor, preferred_element_type=F32) / window]
    psum x1 -> x0, blocking collectives: 40.2 us -> none  [on_device(): first_mode = lax.psum(partial_first, ('wide', 'narrow'))]
    another operation x12, matrix products: 9.24 us -> 3.33 us  [solve_rows(): return jax.scipy.linalg.cho_solve((lower, True), rows.T).T]
    unnamed x11 -> x9, local copies, waits for them, and re-layouts: 6.81 us -> 1.99 us
  transfers between devices with their start and end apart: 2 -> 0, of which waited for: 2 -> 0; matrix products, arithmetic and copies ran while one was open for 0% -> 0% of each run, Pallas kernels for 0% -> 0%
where the time goes in v1:
time: 234 us; the launch traced here: 233 us
  other arithmetic  109 us (47%)
  Pallas kernels  103 us (44%)
  local copies, waits for them, and re-layouts  12.1 us (5%)
  matrix products  5.5 us (2%)
  between operations  3.68 us (2%)
    another operation x13, other arithmetic, solve_rows(): lower = jnp.linalg.cholesky(system)  68.6 us
    another operation x5, other arithmetic, solve_rows(): return jax.scipy.linalg.cho_solve((lower, True), rows.T).T  39.8 us
    pallas_call x1, Pallas kernels, wide_sums(): pl.pallas_call(functools.partial(wide_kernel, size), in_specs=[VM, VM], o...  24.5 us
    pallas_call x1, Pallas kernels, third_products(): pl.pallas_call(third_kernel, grid=(window,), in_specs=[pl.BlockSpec((1, r...  16.6 us
    pallas_call x1, Pallas kernels, narrow_sum(): pl.pallas_call(functools.partial(narrow_kernel, count), in_specs=[VM], ou...  15 us
    pallas_call x1, Pallas kernels, first_products(): pl.pallas_call(first_kernel, grid=(window,), in_specs=[pl.BlockSpec((1, d...  11.8 us
    pallas_call x1, Pallas kernels, second_products(): pl.pallas_call(second_kernel, grid=(window,), in_specs=[pl.BlockSpec((1,...  11.8 us
    pallas_call x1, Pallas kernels, gather_rows(): pl.pallas_call(functools.partial(gather_kernel, size), in_specs=[VM], out...  11.6 us

profile of v1, /device:TPU:0, one launch (start us, length us, event | category | flops | bytes accessed | tf_op | source)
XLA Modules:
  0.0 233.3 jit_solution(9162646859179031779)
XLA Ops:
  1.4 1.0 copy-done.1
  2.4 11.8 %shard_map.58.x_ref = f32[512,256]{1,0:T(8,128)S(1)} custom-call(bf16[16,256,1024]{2,1,0:T(8,128)(2,1)} %t_ref.3, f32[16,1,256]{2,1,0:T(1,128)S(1)} %reshape.91.u_ref, bf16[1024,256]{1,0:T(8,128)(2,1)S(1)} %copy-done.1), custom_call_target="tpu_custom_call" | custom-call | tf_op jit(solution)/shard_map/pallas_call | solution.py:63
  14.2 15.0 %shard_map.59 = f32[512,256]{1,0:T(8,128)S(1)} custom-call(f32[512,256]{1,0:T(8,128)S(1)} %shard_map.58.x_ref), custom_call_target="tpu_custom_call" | custom-call | tf_op jit(solution)/shard_map/pallas_call | solution.py:88
  29.4 1.0 select_add_fusion.1
  30.6 11.7 %cholesky.130 = f32[128,128]{1,0:T(8,128)S(1)} custom-call(f32[128,128]{1,0:T(8,128)S(1)} %cholesky.194), custom_call_target="Cholesky" | custom-call | tf_op jit(solution)/shard_map/jit(cholesky)/cholesky | solution.py:306
  42.5 9.8 %custom-call.25 = f32[1,128,128]{1,2,0:T(8,128)S(1)} custom-call(f32[1,128,128]{2,1,0:T(8,128)S(1)} %get-tuple-element.61), custom_call_target="InvertDiagBlocksLowerTriangular" | custom-call | tf_op jit(solution)/shard_map/jit(cholesky)/cholesky | solution.py:306
  52.9 11.7 %cholesky.147 = f32[128,128]{1,0:T(8,128)S(1)} custom-call(f32[128,128]{1,0:T(8,128)S(1)} %convolution_subtract_fusion.3), custom_call_target="Cholesky" | custom-call | tf_op jit(solution)/shard_map/jit(cholesky)/cholesky | solution.py:306
  66.9 4.3 %while.2 = (s32[]{:T(128)}, f32[256,256]{0,1:T(8,128)S(1)}, s32[2,2]{1,0:T(2,128)S(1)}, f32[2,128,128]{2,1,0:T(8,128)S(1)}, s32[]{:T(128)}) while((s32[]{:T(128)}, f32[256,256]{0,1:T(8,128)S(1)}, s32[2,2]{1,0:T(2,128)S(1)}, f32[2,128,128]{2,1,0:T(8,128)S(1)}, s32[]{:T(128)}) %tuple.46), condition=%wide.while_cond, body=%wide.while_body.sunk | while | flops 2 | bytes 393329 | solution.py:307
  67.5 1.4 dynamic-slice.13
  69.7 1.4 dynamic-slice.13
  71.3 19.9 %custom-call.22 = f32[2,128,128]{1,2,0:T(8,128)S(1)} custom-call(f32[2,128,128]{2,1,0:T(8,128)S(1)} %get-tuple-element.19), custom_call_target="InvertDiagBlocksLowerTriangular" | custom-call | tf_op jit(solution)/shard_map/jit(_cho_solve)/triangular_solve | solution.py:307
  93.5 16.6 %shard_map.60 = (f32[16,1024,256]{2,1,0:T(8,128)}, f32[1024,256]{1,0:T(8,128)S(1)}) custom-call(bf16[16,256,1024]{2,1,0:T(8,128)(2,1)} %t_ref.3, f32[16,1,256]{2,1,0:T(1,128)S(1)} %reshape.91.u_ref, bf16[256,256]{1,0:T(8,128)(2,1)S(1)} %fusion.5.v_ref), custom_call_target="tpu_custom_call" | custom-call | tf_op jit(solution)/shard_map/pallas_call | solution.py:120
  110.1 24.5 %shard_map.61 = (f32[256,256]{1,0:T(8,128)S(1)}, f32[64,256]{1,0:T(8,128)S(1)}) custom-call(f32[256,256]{1,0:T(8,128)S(1)} %fusion.4.gram_ref, f32[1024,256]{1,0:T(8,128)S(1)} %get-tuple-element.8.prod_ref), custom_call_target="tpu_custom_call" | custom-call | tf_op jit(solution)/shard_map/pallas_call | solution.py:194
  134.9 11.7 %cholesky.164 = f32[128,128]{1,0:T(8,128)S(1)} custom-call(f32[128,128]{1,0:T(8,128)S(1)} %cholesky.197), custom_call_target="Cholesky" | custom-call | tf_op jit(solution)/shard_map/jit(cholesky)/cholesky | solution.py:306
  146.8 9.8 %custom-call.26 = f32[1,128,128]{1,2,0:T(8,128)S(1)} custom-call(f32[1,128,128]{2,1,0:T(8,128)S(1)} %get-tuple-element.59), custom_call_target="InvertDiagBlocksLowerTriangular" | custom-call | tf_op jit(solution)/shard_map/jit(cholesky)/cholesky | solution.py:306
  157.2 11.7 %cholesky.181 = f32[128,128]{1,0:T(8,128)S(1)} custom-call(f32[128,128]{1,0:T(8,128)S(1)} %convolution_subtract_fusion.2), custom_call_target="Cholesky" | custom-call | tf_op jit(solution)/shard_map/jit(cholesky)/cholesky | solution.py:306
  171.6 4.1 %while.3 = (s32[]{:T(128)}, f32[256,256]{0,1:T(8,128)S(1)}, s32[2,2]{1,0:T(2,128)S(1)}, f32[2,128,128]{2,1,0:T(8,128)S(1)}, s32[]{:T(128)}) while((s32[]{:T(128)}, f32[256,256]{0,1:T(8,128)S(1)}, s32[2,2]{1,0:T(2,128)S(1)}, f32[2,128,128]{2,1,0:T(8,128)S(1)}, s32[]{:T(128)}) %tuple.54), condition=%wide.while_cond.1, body=%wide.while_body.1.sunk | while | flops 2 | bytes 393329 | solution.py:307
  172.2 1.3 dynamic-slice.15
  174.3 1.3 dynamic-slice.15
  175.7 19.9 %custom-call.23 = f32[2,128,128]{1,2,0:T(8,128)S(1)} custom-call(f32[2,128,128]{2,1,0:T(8,128)S(1)} %get-tuple-element.27), custom_call_target="InvertDiagBlocksLowerTriangular" | custom-call | tf_op jit(solution)/shard_map/jit(_cho_solve)/triangular_solve | solution.py:307
  197.1 11.6 %shard_map.62.z_ref = bf16[1024,256]{1,0:T(8,128)(2,1)S(1)} custom-call(bf16[64,256]{1,0:T(8,128)(2,1)S(1)} %maximum_bitcast_fusion.x_ref), custom_call_target="tpu_custom_call" | custom-call | tf_op jit(solution)/shard_map/pallas_call | solution.py:233
  208.7 11.8 %shard_map.63 = f32[16,1,256]{2,1,0:T(1,128)S(1)} custom-call(f32[16,1024,256]{2,1,0:T(8,128)} %get-tuple-element.11.mid_ref, bf16[1024,256]{1,0:T(8,128)(2,1)S(1)} %shard_map.62.z_ref), custom_call_target="tpu_custom_call" | custom-call | tf_op jit(solution)/shard_map/pallas_call | solution.py:252
  220.6 11.3 %shard_map.64 = f32[16,256]{1,0:T(8,128)S(1)} custom-call(f32[16,256]{1,0:T(8,128)S(1)} %bitcast.83), custom_call_target="tpu_custom_call" | custom-call | tf_op jit(solution)/shard_map/pallas_call | solution.py:289
  232.5 0.8 copy.56
  (78 shorter events, 12.3 us)
Async XLA Ops:
  1.3 1.0 copy-start.1
  93.2 127.3 %copy-start = (bf16[256,256]{1,0:T(8,128)(2,1)}, bf16[256,256]{1,0:T(8,128)(2,1)S(1)}, u32[]{:S(2)}) copy-start(bf16[256,256]{1,0:T(8,128)(2,1)S(1)} %fusion.5.v_ref) | copy-start | bytes 393220

commit v2 on v1

--- a/solution.py
+++ b/solution.py
@@ -44,28 +44,35 @@
 def second_kernel(t_ref, u_ref, w_ref, out_ref):
     step = pl.program_id(0)
     rank = w_ref.shape[1]
+    slabs, rows, depth = t_ref.shape
+    here = pl.ds(rank, rows)
 
     @pl.when(step == 0)
     def _():
         out_ref[pl.ds(0, rank), :] = lax.dot_general(
             w_ref[...], w_ref[...], (((0,), (0,)), ((), ())), preferred_element_type=F32
         )
-        out_ref[pl.ds(rank, t_ref.shape[1]), :] = jnp.zeros((t_ref.shape[1], rank), F32)
-
-    out_ref[pl.ds(rank, t_ref.shape[1]), :] += u_ref[0] * jnp.dot(
-        t_ref[0], w_ref[...], preferred_element_type=F32
-    )
+        out_ref[here, :] = jnp.zeros((rows, rank), F32)
+
+    product = jnp.dot(
+        t_ref[...].reshape(slabs * rows, depth), w_ref[...], preferred_element_type=F32
+    ).reshape(slabs, rows, rank)
+    total = out_ref[here, :]
+    for s in range(slabs):
+        total += u_ref[s] * product[s]
+    out_ref[here, :] = total
 
 
 def second_products(tensor, first_wide, third):
     window, rows, depth = tensor.shape
     rank = third.shape[1]
+    slabs = math.gcd(window, 4)
     return pl.pallas_call(
         second_kernel,
-        grid=(window,),
+        grid=(window // slabs,),
         in_specs=[
-            pl.BlockSpec((1, rows, depth), lambda i: (i, 0, 0)),
-            pl.BlockSpec((1, 1, rank), lambda i: (i, 0, 0)),
+            pl.BlockSpec((slabs, rows, depth), lambda i: (i, 0, 0)),
+            pl.BlockSpec((slabs, 1, rank), lambda i: (i, 0, 0)),
             pl.BlockSpec((depth, rank), lambda i: (0, 0)),
         ],
         out_specs=pl.BlockSpec((rank + rows, rank), lambda i: (0, 0)),
@@ -98,43 +105,47 @@
     )(x)
 
 
-def third_kernel(t_ref, u_ref, v_ref, mid_ref, out_ref):
+def third_kernel(t_ref, u_ref, v_ref, mid_ref, out_ref, acc):
     step = pl.program_id(0)
-    part = lax.dot_general(
-        t_ref[0], v_ref[...], (((0,), (0,)), ((), ())), preferred_element_type=F32
-    )
-    mid_ref[0] = part
 
     @pl.when(step == 0)
     def _():
-        out_ref[...] = u_ref[0] * part
-
-    @pl.when(step > 0)
+        acc[...] = jnp.zeros(acc.shape, F32)
+
+    turned = v_ref[...]
+    for s in range(t_ref.shape[0]):
+        part = jnp.dot(turned, t_ref[s], preferred_element_type=F32)
+        mid_ref[s] = part.astype(BF16)
+        acc[...] += u_ref[s] * part
+
+    @pl.when(step == pl.num_programs(0) - 1)
     def _():
-        out_ref[...] += u_ref[0] * part
-
-
-def third_products(tensor, first_wide, second):
+        out_ref[...] = acc[...].T
+
+
+def third_products(tensor, first_tall, second_turned):
     window, rows, depth = tensor.shape
-    rank = second.shape[1]
+    rank = second_turned.shape[0]
+    slabs = math.gcd(window, 2)
     return pl.pallas_call(
         third_kernel,
-        grid=(window,),
+        grid=(window // slabs,),
         in_specs=[
-            pl.BlockSpec((1, rows, depth), lambda i: (i, 0, 0)),
-            pl.BlockSpec((1, 1, rank), lambda i: (i, 0, 0)),
-            pl.BlockSpec((rows, rank), lambda i: (0, 0)),
+            pl.BlockSpec((slabs, rows, depth), lambda i: (i, 0, 0)),
+            pl.BlockSpec((slabs, rank, 1), lambda i: (i, 0, 0)),
+            pl.BlockSpec((rank, rows), lambda i: (0, 0)),
         ],
         out_specs=[
-            pl.BlockSpec((1, depth, rank), lambda i: (i, 0, 0)),
+            pl.BlockSpec((slabs, rank, depth), lambda i: (i, 0, 0)),
             pl.BlockSpec((depth, rank), lambda i: (0, 0)),
         ],
         out_shape=[
-            jax.ShapeDtypeStruct((window, depth, rank), F32),
+            jax.ShapeDtypeStruct((window, rank, depth), BF16),
             jax.ShapeDtypeStruct((depth, rank), F32),
         ],
+        scratch_shapes=[pltpu.VMEM((rank, depth), F32)],
         compiler_params=params(),
-    )(tensor, first_wide, second)
+    )(tensor, first_tall, second_turned)
 
 
 def place(size):
@@ -244,20 +255,26 @@
 
 
 def first_kernel(mid_ref, z_ref, out_ref):
-    out_ref[0] = jnp.sum(mid_ref[0] * z_ref[...].astype(F32), axis=0, keepdims=True)
+    turned = z_ref[...].astype(F32).T
+    sums = [
+        jnp.sum(mid_ref[s].astype(F32) * turned, axis=1, keepdims=True)
+        for s in range(mid_ref.shape[0])
+    ]
+    out_ref[0] = jnp.concatenate(sums, axis=1).T
 
 
 def first_products(middle, third_new):
-    window, depth, rank = middle.shape
+    window, rank, depth = middle.shape
+    slabs = math.gcd(window, 4)
     return pl.pallas_call(
         first_kernel,
-        grid=(window,),
+        grid=(window // slabs,),
         in_specs=[
-            pl.BlockSpec((1, depth, rank), lambda i: (i, 0, 0)),
+            pl.BlockSpec((slabs, rank, depth), lambda i: (i, 0, 0)),
             pl.BlockSpec((depth, rank), lambda i: (0, 0)),
         ],
-        out_specs=pl.BlockSpec((1, 1, rank), lambda i: (i, 0, 0)),
-        out_shape=jax.ShapeDtypeStruct((window, 1, rank), F32),
+        out_specs=pl.BlockSpec((1, slabs, rank), lambda i: (i, 0, 0)),
+        out_shape=jax.ShapeDtypeStruct((window // slabs, slabs, rank), F32),
         compiler_params=params(),
     )(middle, third_new)
 
@@ -302,9 +319,103 @@
     )(x)
 
 
-def solve_rows(rows, system):
-    lower = jnp.linalg.cholesky(system)
-    return jax.scipy.linalg.cho_solve((lower, True), rows.T).T
+GROUP = 8
+
+
+def split(x):
+    high = x.astype(BF16)
+    rest = x - high.astype(F32)
+    middle = rest.astype(BF16)
+    return high, middle, (rest - middle.astype(F32)).astype(BF16)
+
+
+def eliminate(rows, groups, at):
+    shape = rows[0].shape
+    width = 128
+    lane = lax.broadcasted_iota(jnp.int32, shape, 1)
+    sub = lax.broadcasted_iota(jnp.int32, shape, 0)
+    narrow_sub = lax.broadcasted_iota(jnp.int32, (GROUP, width), 0)
+    for a in range(groups):
+        start = at + a * GROUP
+        own = (lane >= start) & (lane < start + GROUP)
+        columns = [
+            jnp.broadcast_to(rows[a][:, start + j:start + j + 1], (GROUP, width)) for j in range(GROUP)
+        ]
+        target = jnp.where(own, jnp.where(lane - start == sub, 1.0, 0.0), rows[a])
+        for j in range(GROUP):
+            pivot = 1.0 / jnp.broadcast_to(columns[j][j:j + 1], (GROUP, width))
+            factor = jnp.where(narrow_sub == j, -1.0, columns[j]) * pivot
+            for l in range(j + 1, GROUP):
+                row = jnp.broadcast_to(columns[l][j:j + 1], (GROUP, width))
+                columns[l] = jnp.where(narrow_sub == j, 0.0, columns[l]) - factor * row
+            wide = jnp.concatenate([factor] * (shape[1] // width), axis=1)
+            row = jnp.broadcast_to(target[j:j + 1], shape)
+            target = jnp.where(sub == j, 0.0, target) - wide * row
+        for b in range(groups):
+            if b != a:
+                other = jnp.where(own, 0.0, rows[b])
+                for j in range(GROUP):
+                    other -= rows[b][:, start + j:start + j + 1] * target[j:j + 1]
+                rows[b] = other
+        rows[a] = target
+    return rows
+
+
+def invert(ref):
+    size = ref.shape[0]
+    panel = 32
+    groups = panel // GROUP
+    for at in range(0, size, panel):
+        before = ref[pl.ds(at, panel), :]
+        rows = eliminate(
+            [before[g * GROUP:(g + 1) * GROUP] for g in range(groups)], groups, at
+        )
+        after = jnp.concatenate(rows, axis=0)
+        lane = lax.broadcasted_iota(jnp.int32, before.shape, 1)
+        h, m, l = split(jnp.where(lane < at, -before, before))
+        left = jnp.concatenate([h, h, m, m, h, l], axis=0)
+        h, m, l = split(after)
+        right = jnp.concatenate([h, m, h, m, l, h], axis=0)
+        update = lax.dot_general(
+            left, right, (((0,), (0,)), ((), ())), preferred_element_type=F32
+        )
+        column = lax.broadcasted_iota(jnp.int32, (size, size), 1)
+        inside = (column >= at) & (column < at + panel)
+        ref[...] = jnp.where(inside, 0.0, ref[...]) - update
+        ref[pl.ds(at, panel), :] = after
+
+
+def solve_kernel(gram_scale, row_scale, ridge, u_ref, gram_ref, rows_ref, out_ref, local_ref, work):
+    window = u_ref.shape[0]
+    gram_first = lax.dot_general(
+        u_ref[...], u_ref[...], (((0,), (0,)), ((), ())), preferred_element_type=F32
+    ) * (1.0 / window)
+    shape = work.shape
+    diagonal = lax.broadcasted_iota(jnp.int32, shape, 0) == lax.broadcasted_iota(jnp.int32, shape, 1)
+    system = gram_first * (gram_ref[...] * gram_scale)
+    work[...] = jnp.where(diagonal, system + ridge, system)
+    invert(work)
+    out = jnp.dot(
+        rows_ref[...] * row_scale, work[...], preferred_element_type=F32, precision=HIGH
+    ).astype(BF16)
+    out_ref[...] = out
+    local_ref[...] = lax.dot_general(
+        out, out, (((0,), (0,)), ((), ())), preferred_element_type=F32
+    )
+
+def solve(gram_scale, row_scale, first_factor, gram, rows):
+    rank = gram.shape[0]
+    return pl.pallas_call(
+        functools.partial(solve_kernel, gram_scale, row_scale, ridge),
+        in_specs=[VM] * 3,
+        out_specs=[VM] * 2,
+        out_shape=[
+            jax.ShapeDtypeStruct(rows.shape, BF16),
+            jax.ShapeDtypeStruct((rank, rank), F32),
+        ],
+        scratch_shapes=[pltpu.VMEM((rank, rank), F32)],
+        compiler_params=params(),
+    )(first_factor, gram, rows)
 
 
 def on_device(size, count, tensor, first_factor, third_factor):
@@ -313,19 +424,18 @@
     second_total = second_local * size
     third_total = third_local * count
     first_wide = first_factor.astype(F32).reshape(window, 1, rank)
-    identity = jnp.eye(rank, dtype=F32)
-    gram_first = jnp.dot(first_factor.T, first_factor, preferred_element_type=F32) / window
+    first_tall = first_factor.astype(F32).reshape(window, rank, 1)
     sums = narrow_sum(second_products(tensor, first_wide, third_factor), count)
-    gram_third = sums[:rank] / third_total
-    mttkrp_second = sums[rank:] / math.sqrt(window * third_total)
-    system_second = gram_first * gram_third + ridge * identity
-    second_factor = solve_rows(mttkrp_second, system_second).astype(BF16)
-    gram_local = jnp.dot(second_factor.T, second_factor, preferred_element_type=F32)
-    middle, partial_third = third_products(tensor, first_wide, second_factor)
+    second_factor, gram_local = solve(
+        1.0 / third_total, 1.0 / math.sqrt(window * third_total),
+        first_factor, sums[:rank], sums[rank:],
+    )
+    middle, partial_third = third_products(tensor, first_tall, second_factor.T)
     gram_second, rows_third = wide_sums(gram_local, partial_third, size)
-    system_third = gram_first * (gram_second / second_total) + ridge * identity
-    mttkrp_third = rows_third / math.sqrt(window * second_total)
-    third_rows = solve_rows(mttkrp_third, system_third).astype(BF16)
+    third_rows, _ = solve(
+        1.0 / second_total, 1.0 / math.sqrt(window * second_total),
+        first_factor, gram_second, rows_third,
+    )
     third_new = gather_rows(third_rows, size)
     partial_first = first_products(middle, third_new).reshape(window, rank)
     first_mode = total_sum(partial_first, size, count) / math.sqrt(second_total * third_total)

time: 234 us -> 112 us (0.48)
  other arithmetic: 109 us -> 1.37 us
  local copies, waits for them, and re-layouts: 12.1 us -> 4.23 us
  matrix products: 5.5 us -> 0 us
  between operations: 3.68 us -> 0.73 us
    another operation x18 -> x0, other arithmetic: 108 us -> none  [the longest x13 68.6 us: solve_rows(): lower = jnp.linalg.cholesky(system)]
    another operation x36 -> x0, local copies, waits for them, and re-layouts: 9.05 us -> none
    another operation x16 -> x0, matrix products: 4.27 us -> none  [the longest x12 3.33 us: solve_rows(): return jax.scipy.linalg.cho_solve((lower, True), rows.T).T]
    pallas_call x3 -> x5, Pallas kernels: 40.2 us -> 42.8 us  [the longest x2 20.8 us: solve(): pl.pallas_call(functools.partial(solve_kernel, gram_scale, row_scale, rid...]
where the time goes in v2:
time: 112 us; the launch traced here: 111 us
  Pallas kernels  105 us (94%)
  local copies, waits for them, and re-layouts  4.23 us (4%)
  other arithmetic  1.37 us (1%)
    pallas_call x1, Pallas kernels, wide_sums(): pl.pallas_call(functools.partial(wide_kernel, size), in_specs=[VM, VM], o...  24.4 us
    pallas_call x2, Pallas kernels, solve(): pl.pallas_call(functools.partial(solve_kernel, gram_scale, row_scale, rid...  20.8 us
    pallas_call x1, Pallas kernels, narrow_sum(): pl.pallas_call(functools.partial(narrow_kernel, count), in_specs=[VM], ou...  15 us
    pallas_call x1, Pallas kernels, gather_rows(): pl.pallas_call(functools.partial(gather_kernel, size), in_specs=[VM], out...  11.5 us
    pallas_call x1, Pallas kernels, total_sum(): pl.pallas_call(functools.partial(total_kernel, size, count), in_specs=[VM...  11.3 us
    pallas_call x1, Pallas kernels, third_products(): pl.pallas_call(third_kernel, grid=(window // slabs,), in_specs=[pl.BlockS...  10.9 us
    pallas_call x1, Pallas kernels, second_products(): pl.pallas_call(second_kernel, grid=(window // slabs,), in_specs=[pl.Block...  5.86 us
    pallas_call x1, Pallas kernels, first_products(): pl.pallas_call(first_kernel, grid=(window // slabs,), in_specs=[pl.BlockS...  5.33 us

profile of v2, /device:TPU:0, one launch (start us, length us, event | category | flops | bytes accessed | tf_op | source)
XLA Modules:
  0.0 111.4 jit_solution(5868693656245848839)
XLA Ops:
  0.6 0.0 copy-start.1
  0.6 0.8 convert_bitcast_fusion
  1.4 0.7 reshape.15.u_ref
  2.1 0.0 copy-start
  2.1 1.0 copy-done
  3.2 5.9 %shard_map.58.x_ref = f32[512,256]{1,0:T(8,128)S(1)} custom-call(bf16[16,256,1024]{2,1,0:T(8,128)(2,1)} %t_ref.3, f32[16,1,256]{2,1,0:T(1,128)S(1)} %reshape.15.u_ref, bf16[1024,256]{1,0:T(8,128)(2,1)S(1)} %copy-done), custom_call_target="tpu_custom_call" | custom-call | tf_op jit(solution)/shard_map/pallas_call | solution.py:70
  9.0 15.0 %shard_map.59 = f32[512,256]{1,0:T(8,128)S(1)} custom-call(f32[512,256]{1,0:T(8,128)S(1)} %shard_map.58.x_ref), custom_call_target="tpu_custom_call" | custom-call | tf_op jit(solution)/shard_map/pallas_call | solution.py:95
  24.1 0.0 copy-done.1
  24.1 10.4 %shard_map.60 = (bf16[256,256]{1,0:T(8,128)(2,1)}, f32[256,256]{1,0:T(8,128)S(1)}) custom-call(bf16[16,256]{1,0:T(8,128)(2,1)S(1)} %copy-done.1, f32[256,256]{1,0:T(8,128)S(1)} %get-tuple-element.18.gram_ref, f32[256,256]{1,0:T(8,128)S(1)} %get-tuple-element.17.rows_ref), custom_call_target="tpu_custom_call" | custom-call | tf_op jit(solution)/shard_map/pallas_call | solution.py:408
  34.4 1.0 copy.8
  35.5 0.6 copy.9.u_ref
  36.1 10.9 %shard_map.61 = (bf16[16,256,1024]{2,1,0:T(8,128)(2,1)}, f32[1024,256]{1,0:T(8,128)S(1)}) custom-call(bf16[16,256,1024]{2,1,0:T(8,128)(2,1)} %t_ref.3, f32[16,256,1]{2,1,0:T(8,128)S(1)} %copy.9.u_ref, bf16[256,256]{1,0:T(8,128)(2,1)S(1)} %bitcast.3), custom_call_target="tpu_custom_call" | custom-call | tf_op jit(solution)/shard_map/pallas_call | solution.py:130
  47.0 24.4 %shard_map.62 = (f32[256,256]{1,0:T(8,128)S(1)}, f32[64,256]{1,0:T(8,128)S(1)}) custom-call(f32[256,256]{1,0:T(8,128)S(1)} %get-tuple-element.11.gram_ref, f32[1024,256]{1,0:T(8,128)S(1)} %get-tuple-element.12.prod_ref), custom_call_target="tpu_custom_call" | custom-call | tf_op jit(solution)/shard_map/pallas_call | solution.py:205
  71.4 10.4 %shard_map.63 = (bf16[64,256]{1,0:T(8,128)(2,1)S(1)}, f32[256,256]{1,0:T(8,128)}) custom-call(bf16[16,256]{1,0:T(8,128)(2,1)S(1)} %copy-done.1, f32[256,256]{1,0:T(8,128)S(1)} %get-tuple-element.13.gram_ref, f32[64,256]{1,0:T(8,128)S(1)} %get-tuple-element.14.rows_ref), custom_call_target="tpu_custom_call" | custom-call | tf_op jit(solution)/shard_map/pallas_call | solution.py:408
  81.8 11.5 %shard_map.64.z_ref = bf16[1024,256]{1,0:T(8,128)(2,1)S(1)} custom-call(bf16[64,256]{1,0:T(8,128)(2,1)S(1)} %get-tuple-element.15.x_ref), custom_call_target="tpu_custom_call" | custom-call | tf_op jit(solution)/shard_map/pallas_call | solution.py:244
  93.4 5.3 %shard_map.65 = f32[4,4,256]{2,1,0:T(4,128)S(1)} custom-call(bf16[16,256,1024]{2,1,0:T(8,128)(2,1)} %get-tuple-element.16.mid_ref, bf16[1024,256]{1,0:T(8,128)(2,1)S(1)} %shard_map.64.z_ref), custom_call_target="tpu_custom_call" | custom-call | tf_op jit(solution)/shard_map/pallas_call | solution.py:269
  98.7 11.3 %shard_map.66 = f32[16,256]{1,0:T(8,128)S(1)} custom-call(f32[16,256]{1,0:T(8,128)S(1)} %reshape.17.x_ref), custom_call_target="tpu_custom_call" | custom-call | tf_op jit(solution)/shard_map/pallas_call | solution.py:306
  110.0 0.6 broadcast_multiply_fusion
  110.6 0.8 copy.11
  (2 shorter events, 0.0 us)
Async XLA Ops:
  0.6 23.5 %copy-start.1 = (bf16[16,256]{1,0:T(8,128)(2,1)S(1)}, bf16[16,256]{1,0:T(8,128)(2,1)}, u32[]{:S(2)}) copy-start(bf16[16,256]{1,0:T(8,128)(2,1)} %u_ref.3) | copy-start | bytes 24580
  2.1 1.0 copy-start

commit v3 on v0

v3 whole, which is shorter than its diff:
```python
import functools
import math

import jax
import jax.numpy as jnp
from jax import lax
from jax.experimental import pallas as pl
from jax.experimental.pallas import tpu as pltpu
from jax.sharding import PartitionSpec as P

ridge = 0.5
F32 = jnp.float32
BF16 = jnp.bfloat16
HIGH = lax.Precision.HIGHEST
VM = pl.BlockSpec(memory_space=pltpu.VMEM)
MESH = pl.DeviceIdType.MESH


def params(**more):
    return pltpu.CompilerParams(vmem_limit_bytes=50 * 2**20, **more)


def remote(src, dst, sems, slot, wide, narrow):
    copy = pltpu.make_async_remote_copy(
        src_ref=src, dst_ref=dst, send_sem=sems.at[0, slot], recv_sem=sems.at[1, slot],
        device_id=(wide, narrow), device_id_type=MESH,
    )
    copy.start()
    return copy


def greet(partners):
    barrier = pltpu.get_barrier_semaphore()
    for partner in partners:
        pl.semaphore_signal(barrier, inc=1, device_id=partner, device_id_type=MESH)
    pl.semaphore_wait(barrier, len(partners))


def wait_all(copies):
    for copy in copies:
        copy.wait()


GROUP = 8


def split(x):
    high = x.astype(BF16)
    rest = x - high.astype(F32)
    middle = rest.astype(BF16)
    return high, middle, (rest - middle.astype(F32)).astype(BF16)


def eliminate(rows, groups, at):
    shape = rows[0].shape
    width = 128
    lane = lax.broadcasted_iota(jnp.int32, shape, 1)
    sub = lax.broadcasted_iota(jnp.int32, shape, 0)
    narrow_sub = lax.broadcasted_iota(jnp.int32, (GROUP, width), 0)
    for a in range(groups):
        start = at + a * GROUP
        own = (lane >= start) & (lane < start + GROUP)
        columns = [
            jnp.broadcast_to(rows[a][:, start + j:start + j + 1], (GROUP, width)) for j in range(GROUP)
        ]
        target = jnp.where(own, jnp.where(lane - start == sub, 1.0, 0.0), rows[a])
        for j in range(GROUP):
            pivot = 1.0 / jnp.broadcast_to(columns[j][j:j + 1], (GROUP, width))
            factor = jnp.where(narrow_sub == j, -1.0, columns[j]) * pivot
            for l in range(j + 1, GROUP):
                row = jnp.broadcast_to(columns[l][j:j + 1], (GROUP, width))
                columns[l] = jnp.where(narrow_sub == j, 0.0, columns[l]) - factor * row
            wide = jnp.concatenate([factor] * (shape[1] // width), axis=1)
            row = jnp.broadcast_to(target[j:j + 1], shape)
            target = jnp.where(sub == j, 0.0, target) - wide * row
        for b in range(groups):
            if b != a:
                other = jnp.where(own, 0.0, rows[b])
                for j in range(GROUP):
                    other -= rows[b][:, start + j:start + j + 1] * target[j:j + 1]
                rows[b] = other
        rows[a] = target
    return rows


def invert(ref):
    size = ref.shape[0]
    panel = 32
    groups = panel // GROUP

    def step(index, carry):
        at = pl.multiple_of(index * panel, panel)
        before = ref[pl.ds(at, panel), :]
        turned = pltpu.roll(before, size - at, 1)
        rows = eliminate(
            [turned[g * GROUP:(g + 1) * GROUP] for g in range(groups)], groups, 0
        )
        after = pltpu.roll(jnp.concatenate(rows, axis=0), at, 1)
        lane = lax.broadcasted_iota(jnp.int32, before.shape, 1)
        h, m, l = split(jnp.where(lane < at, -before, before))
        left = jnp.concatenate([h, h, m, m, h, l], axis=0)
        h, m, l = split(after)
        right = jnp.concatenate([h, m, h, m, l, h], axis=0)
        update = lax.dot_general(
            left, right, (((0,), (0,)), ((), ())), preferred_element_type=F32
        )
        column = lax.broadcasted_iota(jnp.int32, (size, size), 1)
        inside = (column >= at) & (column < at + panel)
        ref[...] = jnp.where(inside, 0.0, ref[...]) - update
        ref[pl.ds(at, panel), :] = after
        return carry

    lax.fori_loop(0, size // panel, step, 0)


def set_system(work, gram_first, gram):
    shape = work.shape
    diagonal = lax.broadcasted_iota(jnp.int32, shape, 0) == lax.broadcasted_iota(jnp.int32, shape, 1)
    system = gram_first * gram
    work[...] = jnp.where(diagonal, system + ridge, system)


PIECES = 4


def part(ref, index, rows):
    return ref.at[pl.ds(pl.multiple_of(index * rows, rows), rows)]


def sweep(size, count, t_hbm, u_ref, w_ref, second_out, third_out, first_out,
          t_ref, mid, acc, g_src, p_src, g_land, p_land, work,
          gl_src, gl_land, gl_acc, gl_parts, gl_all,
          prod_src, prod_land, prod_acc, prod_parts, z_src,
          f_src, f_land, f_acc, f_parts,
          load_sems, g_sems, p_sems, core_sems, gram_sems, share_sems, prod_sems,
          z_sems, z_core_sems, f_sems):
    wide, narrow = lax.axis_index("wide"), lax.axis_index("narrow")
    chips = size // 2
    chip, core = wide // 2, lax.rem(wide, 2)
    peer = chip * 2 + 1 - core
    others = [lax.rem(chip + d, chips) for d in range(1, chips)]
    across = [lax.rem(narrow + e, count) for e in range(1, count)]
    partners = []
    for d in range(chips):
        for e in range(count):
            if d or e:
                partners.append((lax.rem(chip + d, chips) * 2 + core, lax.rem(narrow + e, count)))

    window, rows, depth = t_ref.shape
    rank = u_ref.shape[1]
    slabs = window // PIECES
    second_total, third_total = rows * size, depth * count
    loads = [
        pltpu.make_async_copy(
            t_hbm.at[pl.ds(c * slabs, slabs)], t_ref.at[pl.ds(c * slabs, slabs)], load_sems.at[c]
        ) for c in range(PIECES)
    ]
    for load in loads:
        load.start()
    greet([(peer, narrow)] + partners)

    g_src[...] = lax.dot_general(
        w_ref[...], w_ref[...], (((0,), (0,)), ((), ())), preferred_element_type=F32
    )
    g_sends = [remote(g_src, g_land.at[d], g_sems, d, wide, e) for d, e in enumerate(across)]
    u_rows = u_ref[...].astype(F32)
    u_columns = u_rows.T
    gram_first = lax.dot_general(
        u_ref[...], u_ref[...], (((0,), (0,)), ((), ())), preferred_element_type=F32
    ) * (1.0 / window)
    for c in range(PIECES):
        loads[c].wait()
        product = jnp.dot(
            t_ref[pl.ds(c * slabs, slabs)].reshape(slabs * rows, depth), w_ref[...],
            preferred_element_type=F32,
        ).reshape(slabs, rows, rank)
        total = product[0] * u_rows[c * slabs:c * slabs + 1]
        for s in range(1, slabs):
            total += product[s] * u_rows[c * slabs + s:c * slabs + s + 1]
        p_src[...] = total if c == 0 else p_src[...] + total
    p_sends = [remote(p_src, p_land.at[d], p_sems, d, wide, e) for d, e in enumerate(across)]
    wait_all(g_sends)
    total = g_src[...]
    for d in range(count - 1):
        total += g_land[d]
    set_system(work, gram_first, total * (1.0 / third_total))
    invert(work)
    wait_all(p_sends)
    total = p_src[...]
    for d in range(count - 1):
        total += p_land[d]
    second = jnp.dot(
        total * (1.0 / math.sqrt(window * third_total)), work[...],
        preferred_element_type=F32, precision=HIGH,
    )
    second_out[...] = second.astype(BF16)
    turned = second.T.astype(BF16)
    gl_src[...] = jnp.dot(turned, second.astype(BF16), preferred_element_type=F32)

    g_half, p_half = rank // 2, depth // 2
    g_rows, p_rows = g_half // chips, p_half // chips

    def middle(first, last):
        for s in range(first, last):
            product = jnp.dot(turned, t_ref[s], preferred_element_type=F32)
            mid[s] = product.astype(BF16)
            scaled = product * u_columns[:, s:s + 1]
            acc[...] = scaled if s == 0 else acc[...] + scaled

    pair = remote(part(gl_src, 1 - core, g_half), gl_land, core_sems, 0, peer, narrow)
    middle(0, window // 4)
    pair.wait()
    gl_acc[...] = part(gl_src, core, g_half)[...] + gl_land[...]
    grams = [remote(part(gl_acc, other, g_rows), gl_parts.at[d], gram_sems, d,
                    other * 2 + core, narrow) for d, other in enumerate(others)]
    middle(window // 4, window * 5 // 8)
    wait_all(grams)
    total = part(gl_acc, chip, g_rows)[...]
    for d in range(chips - 1):
        total += gl_parts[d]
    mine = part(gl_all, core * chips + chip, g_rows)
    mine[...] = total
    shares = [remote(mine, mine, share_sems, d, other * 2 + core, narrow)
              for d, other in enumerate(others)]
    middle(window * 5 // 8, window)
    prod_src[...] = acc[...].T
    halves = remote(part(prod_src, 1 - core, p_half), prod_land, core_sems, 1, peer, narrow)
    wait_all(shares)
    half = part(gl_all, core, g_half)
    pair = remote(half, half, core_sems, 2, peer, narrow)
    halves.wait()
    prod_acc[...] = part(prod_src, core, p_half)[...] + prod_land[...]
    prods = [remote(part(prod_acc, other, p_rows), prod_parts.at[d], prod_sems, d,
                    other * 2 + core, narrow) for d, other in enumerate(others)]
    pair.wait()

    set_system(work, gram_first, gl_all[...] * (1.0 / second_total))
    invert(work)
    wait_all(prods)
    total = part(prod_acc, chip, p_rows)[...]
    for d in range(chips - 1):
        total += prod_parts[d]
    z_src[...] = jnp.dot(
        total * (1.0 / math.sqrt(window * second_total)), work[...],
        preferred_element_type=F32, precision=HIGH,
    ).astype(BF16)
    mine = part(third_out, core * chips + chip, p_rows)
    sends = [remote(z_src, mine, z_sems, d, other * 2 + core, narrow)
             for d, other in enumerate(others)]
    passes = [remote(z_src, mine, z_core_sems, 0, peer, narrow)]
    mine[...] = z_src[...]
    for d in range(1, chips):
        sends[d - 1].wait()
        block = part(third_out, core * chips + lax.rem(chip + chips - d, chips), p_rows)
        passes.append(remote(block, block, z_core_sems, d, peer, narrow))
    wait_all(passes)

    turned = third_out[...].astype(F32).T
    sums = [
        jnp.sum(mid[s].astype(F32) * turned, axis=1, keepdims=True) for s in range(window)
    ]
    f_src[...] = jnp.concatenate(sums, axis=1).T
    f_half = window // 2
    remote(part(f_src, 1 - core, f_half), f_land, core_sems, 3, peer, narrow).wait()
    f_acc[...] = part(f_src, core, f_half)[...] + f_land[...]
    wait_all([remote(f_acc, f_parts.at[d], f_sems, d, *partner)
              for d, partner in enumerate(partners)])
    total = f_acc[...]
    for d in range(len(partners)):
        total += f_parts[d]
    mine = part(first_out, core, f_half)
    mine[...] = total * (1.0 / math.sqrt(second_total * third_total))
    remote(mine, mine, core_sems, 4, peer, narrow).wait()


def on_device(size, count, tensor, first_factor, third_factor):
    window, rows, depth = tensor.shape
    rank = first_factor.shape[1]
    chips = size // 2
    partners = chips * count - 1
    g_rows, p_rows = rank // size, depth // size
    dma = pltpu.SemaphoreType.DMA

    def floats(*shape):
        return pltpu.VMEM(shape, F32)

    return pl.pallas_call(
        functools.partial(sweep, size, count),
        in_specs=[pl.BlockSpec(memory_space=pl.ANY), VM, VM],
        out_specs=[VM] * 3,
        out_shape=[
            jax.ShapeDtypeStruct((rows, rank), BF16),
            jax.ShapeDtypeStruct((depth, rank), BF16),
            jax.ShapeDtypeStruct((window, rank), F32),
        ],
        scratch_shapes=[
            pltpu.VMEM((window, rows, depth), BF16), pltpu.VMEM((window, rank, depth), BF16),
            floats(rank, depth), floats(rank, rank), floats(rows, rank),
            floats(count - 1, rank, rank), floats(count - 1, rows, rank), floats(rank, rank),
            floats(rank, rank), floats(rank // 2, rank), floats(rank // 2, rank),
            floats(chips - 1, g_rows, rank), floats(rank, rank),
            floats(depth, rank), floats(depth // 2, rank), floats(depth // 2, rank),
            floats(chips - 1, p_rows, rank), pltpu.VMEM((p_rows, rank), BF16),
            floats(window, rank), floats(window // 2, rank), floats(window // 2, rank),
            floats(partners, window // 2, rank),
            dma((PIECES,)), dma((2, count - 1)), dma((2, count - 1)), dma((2, 5)),
            dma((2, chips - 1)), dma((2, chips - 1)), dma((2, chips - 1)),
            dma((2, chips - 1)), dma((2, chips)), dma((2, partners)),
        ],
        compiler_params=params(collective_id=0, has_side_effects=True),
    )(tensor, first_factor, third_factor)


def solution(mesh):
    size, count = mesh.shape["wide"], mesh.shape["narrow"]
    in_specs = (P(None, "wide", "narrow"), P(), P("narrow", None))
    out_specs = (P("wide", None), P("narrow", None), P())
    return jax.shard_map(
        functools.partial(on_device, size, count), mesh=mesh,
        in_specs=in_specs, out_specs=out_specs, check_vma=False,
    )
```

time: 384 us -> 72.5 us (0.19)
  waiting for transfers between devices: 124 us -> 0 us
  other arithmetic: 112 us -> 0 us
  matrix products: 70.3 us -> 0 us
  Pallas kernels: 0 us -> 67.9 us
  blocking collectives: 40.2 us -> 0 us
  between operations: 17.1 us -> 0.65 us
  local copies, waits for them, and re-layouts: 16.1 us -> 3.79 us
    psum x2 -> x0, waiting for transfers between devices: 124 us -> none  [the longest x1 93.1 us: on_device(): mttkrp_third = lax.psum(partial_third, 'wide')]
    another operation x18 -> x0, other arithmetic: 108 us -> none  [the longest x13 68.6 us: solve_rows(): lower = jnp.linalg.cholesky(system)]
    pallas_call x0 -> x1, Pallas kernels: none -> 67.9 us  [on_device(): pl.pallas_call(functools.partial(sweep, size, count), in_specs=[pl.BlockS...]
    dot_general x7 -> x0, matrix products: 60.1 us -> none  [the longest x1 32 us: on_device(): jnp.einsum('ikr,kr->ir', middle, third_solution, precision=lax.Precision....]
    psum x1 -> x0, blocking collectives: 40.2 us -> none  [on_device(): first_mode = lax.psum(partial_first, ('wide', 'narrow'))]
    another operation x16 -> x0, matrix products: 10.2 us -> none  [the longest x12 9.24 us: solve_rows(): return jax.scipy.linalg.cho_solve((lower, True), rows.T).T]
    another operation x35 -> x0, local copies, waits for them, and re-layouts: 8.79 us -> none
  transfers between devices with their start and end apart: 2 -> 0, of which waited for: 2 -> 0; matrix products, arithmetic and copies ran while one was open for 0% -> 0% of each run, Pallas kernels for 0% -> 0%
where the time goes in v3:
time: 72.5 us; the launch traced here: 72.3 us
  Pallas kernels  67.9 us (94%)
  local copies, waits for them, and re-layouts  3.79 us (5%)
    pallas_call x1, Pallas kernels, on_device(): pl.pallas_call(functools.partial(sweep, size, count), in_specs=[pl.BlockS...  67.9 us
    unnamed x7, local copies, waits for them, and re-layouts  3.79 us

profile of v3, /device:TPU:0, one launch (start us, length us, event | category | flops | bytes accessed | tf_op | source)
XLA Modules:
  0.0 72.3 jit_solution(8427995581373537441)
XLA Ops:
  0.6 0.0 copy-start
  0.6 1.0 %copy-done = bf16[1024,256]{1,0:T(8,128)(2,1)S(1)} copy-done((bf16[1024,256]{1,0:T(8,128)(2,1)S(1)}, bf16[1024,256]{1,0:T(8,128)(2,1)}, u32[]{:S(2)}) %copy-start) | copy-done | bytes 524312
  1.7 0.0 copy-start.1
  1.7 0.7 copy-done.1
  2.4 67.9 %shard_map.58 = (bf16[256,256]{1,0:T(8,128)(2,1)S(1)}, bf16[1024,256]{1,0:T(8,128)(2,1)S(1)}, f32[16,256]{1,0:T(8,128)S(1)}) custom-call(bf16[16,256,1024]{2,1,0:T(8,128)(2,1)} %t_hbm.1, bf16[16,256]{1,0:T(8,128)(2,1)S(1)} %copy-done.1, bf16[1024,256]{1,0:T(8,128)(2,1)S(1)} %copy-done), custom_call_target="tpu_custom_call" | custom-call | tf_op jit(solution)/shard_map/pallas_call | solution.py:287
  70.3 0.7 copy.9
  70.9 0.8 %copy.10 = bf16[1024,256]{1,0:T(8,128)(2,1)} copy(bf16[1024,256]{1,0:T(8,128)(2,1)S(1)} %get-tuple-element.7) | data formatting | bytes 1048576
  71.7 0.6 copy.11
Async XLA Ops:
  0.6 1.0 %copy-start = (bf16[1024,256]{1,0:T(8,128)(2,1)S(1)}, bf16[1024,256]{1,0:T(8,128)(2,1)}, u32[]{:S(2)}) copy-start(bf16[1024,256]{1,0:T(8,128)(2,1)} %w_ref.1) | copy-start | bytes 1572868
  1.7 0.7 copy-start.1
